TPU v7x, 32 devices: a whole 2x2x4 slice. The times are simulated.
32 devices in a mesh: groups: 2 (over y), loop: 4 (over z), enc: 2 (over x), rep: 2 (over core).
Axes of the slice: x: 2, y: 2, z: 4, core: 2. Of those that a mesh axis runs over, the one named last changes fastest.
Arguments:
- embeddings: bfloat16 [4096, 768], P(('groups', 'loop', 'rep'), 'enc'), parts along dimension 0, may hold values from -24 to 24
- head_weight: bfloat16 [768, 768], P('enc'), may hold values from -0.21875 to 0.21875
- gp_weights: float32 [4096], P('groups'), parts along dimension 0, may hold values from -24 to 24
- counts: int32 [8], P('groups'), parts along dimension 0, may hold values from 64 to 512, as said below
Outputs:
- embed_grad: bfloat16 [4096, 768], P(('groups', 'loop', 'rep'), 'enc'), parts along dimension 0
- head_grad: float32 [1536, 768], P(('groups', 'enc')), parts along dimension 0
There are 2 independent parts, one for each index of `groups`. A program takes and returns all parts, laid end to end along the dimension named above; an argument that names none is the same for every part. Nothing has to cross between parts.
Inputs may be any that keep to these rules, and one draw needn't show every extreme that they name: `counts`: some block is full and some block holds exactly 64 valid molecules.
All inputs are finite; a program needn't handle non-finite values.
Results may differ from a plain program's by a relative error of at most 0.019.
Values may be sent and summed in bfloat16 or wider, within the bound.
A program may use at most 64 MiB of HBM per device.

v0:
```python
import jax
import jax.numpy as jnp
from jax import lax
from jax.sharding import PartitionSpec as P

EPSILON = 1e-06


def passed_along(value, axis, steps):
    count = lax.axis_size(axis)
    pairs = [(source, (source + steps) % count) for source in range(count)]
    return lax.ppermute(value, axis, pairs)


def pass_forward(piece):
    return passed_along(piece, "loop", 1)


def body(embeddings, head_weight, gp_weights, counts):
    enc_size = lax.axis_size("enc")
    rep_size = lax.axis_size("rep")
    loop_size = lax.axis_size("loop")
    share_rows = embeddings.shape[0]
    piece_rows = share_rows // enc_size
    block_rows = share_rows * rep_size
    loop_index = lax.axis_index("loop")
    enc_index = lax.axis_index("enc")
    rep_index = lax.axis_index("rep")
    rows = embeddings
    own_feats = lax.psum_scatter(
        jnp.dot(rows, head_weight, preferred_element_type=jnp.float32),
        "enc",
        scatter_dimension=0,
        tiled=True,
    ).astype(jnp.bfloat16)
    block_feats = lax.all_gather(own_feats, ("enc", "rep"), axis=0, tiled=True)
    block_norms = jnp.sum(jnp.square(block_feats.astype(jnp.float32)), axis=1)
    offsets = (
        jnp.arange(rep_size, dtype=jnp.int32)[None, :, None] * share_rows
        + jnp.arange(enc_size, dtype=jnp.int32)[:, None, None] * piece_rows
        + jnp.arange(piece_rows, dtype=jnp.int32)[None, None, :]
    ).reshape(block_rows)
    own_base = lax.dynamic_slice_in_dim(gp_weights, loop_index * block_rows, block_rows)
    block_coef = (
        own_base.reshape(rep_size, enc_size, piece_rows).transpose(1, 0, 2).reshape(block_rows)
    )
    own_count = lax.dynamic_index_in_dim(counts, loop_index, keepdims=False)
    block_coef = jnp.where(offsets < own_count, block_coef, 0.0)
    piece_start = rep_index * share_rows + enc_index * piece_rows
    piece_offsets = piece_start + jnp.arange(piece_rows, dtype=jnp.int32)

    def tile(state, piece, anchor):
        anchor_count = lax.dynamic_index_in_dim(counts, anchor, keepdims=False)
        accum, quotient_sum = state
        piece_coef = lax.dynamic_slice_in_dim(
            gp_weights, anchor * block_rows + piece_start, piece_rows
        )
        piece_coef = jnp.where(piece_offsets < anchor_count, piece_coef, 0.0)
        piece_norms = jnp.sum(jnp.square(piece.astype(jnp.float32)), axis=1)
        scores = lax.dot_general(
            piece, block_feats, (((1,), (1,)), ((), ())), preferred_element_type=jnp.float32
        )
        denom = piece_norms[:, None] + block_norms[None, :] - scores + EPSILON
        inverse = 1.0 / (denom * denom)
        pair_coef = piece_coef[:, None] * block_coef[None, :]
        pair_weight = (pair_coef * (piece_norms[:, None] + block_norms[None, :]) * inverse).astype(
            jnp.bfloat16
        )
        quotient_sum = quotient_sum + jnp.sum(pair_coef * 2.0 * scores * inverse, axis=0)
        accum = accum + lax.dot_general(
            pair_weight, piece, (((0,), (0,)), ((), ())), preferred_element_type=jnp.float32
        )
        return (accum, quotient_sum)

    start_state = (
        jnp.zeros((block_rows, block_feats.shape[1]), jnp.float32),
        jnp.zeros((block_rows,), jnp.float32),
    )
    state = tile(start_state, own_feats, loop_index)

    def forward_step(step_index, carry):
        moving, inner = carry
        moving = pass_forward(moving)
        inner = tile(inner, moving, (loop_index - step_index - 1 + loop_size) % loop_size)
        return (moving, inner)

    moving, state = lax.fori_loop(0, loop_size - 1, forward_step, (own_feats, state))
    accum, quotient_sum = state
    grad_block = accum - block_feats.astype(jnp.float32) * quotient_sum[:, None]
    own_grad = lax.psum_scatter(
        grad_block.astype(jnp.bfloat16), ("enc", "rep"), scatter_dimension=0, tiled=True
    )
    piece = lax.all_gather(own_grad, "enc", axis=0, tiled=True)
    back = lax.dot_general(
        piece, head_weight, (((1,), (1,)), ((), ())), preferred_element_type=jnp.float32
    )
    embed_part = back
    rows = embeddings
    head_part = lax.dot_general(
        rows, piece, (((0,), (0,)), ((), ())), preferred_element_type=jnp.float32
    )
    embed_part, head_part = (embed_part, head_part)
    head_grad = lax.psum(head_part, ("loop", "rep"))
    return (embed_part.astype(jnp.bfloat16), head_grad)


def solution(mesh):
    placed = (P(("groups", "loop", "rep"), "enc"), P("enc", None), P("groups"), P("groups"))
    return jax.shard_map(
        body,
        mesh=mesh,
        in_specs=placed,
        out_specs=(P(("groups", "loop", "rep"), "enc"), P(("groups", "enc"), None)),
        check_vma=False,
    )
```

profile of v0, /device:TPU:0, one launch (start us, length us, event | category | flops | bytes accessed | tf_op | source)
XLA Modules:
  0.0 170.0 jit_solution(11172648524668776611)
XLA Ops:
  7.2 1.0 copy-done
  8.2 2.2 %fusion.40 = f32[256,768]{1,0:T(8,128)} fusion(bf16[256,384]{1,0:T(8,128)(2,1)} %param.6, bf16[384,768]{1,0:T(8,128)(2,1)S(1)} %copy-done), kind=kOutput, calls=%fused_computation.56 | convolution fusion | flops 150994944 | bytes 1572864 | tf_op jit(solution)/shard_map/dot_general | solution.py:31
  10.5 0.7 dynamic_slice.37
  11.2 0.8 dynamic_slice.39
  12.0 0.8 compare_select_fusion.1
  12.8 1.5 compare_select_fusion.2
  14.2 16.8 %reduce-scatter.3.cloned.1.call-done = f32[128,768]{1,0:T(8,128)} async-done(((f32[256,768]{1,0:T(8,128)}), f32[128,768]{1,0:T(8,128)}) %reduce-scatter.3.cloned.1.call-update) | async-done | bytes 393232 | tf_op jit(solution)/shard_map/reduce_scatter | solution.py:30
  31.0 1.1 multiply_reduce_fusion.1
  32.1 8.2 %all_gather.6 = bf16[512,768]{1,0:T(8,128)(2,1)S(1)} all-gather(bf16[128,768]{1,0:T(8,128)(2,1)S(1)} %get-tuple-element.541), channel_id=1, replica_groups=mesh['groups'=2,'loop'=4,'enc'=2,'rep'=2] {'enc','rep'}, dimensions={0}, use_global_device_ids=true | all-gather | bytes 983040 | tf_op jit(solution)/shard_map/all_gather | solution.py:36
  41.0 0.5 fusion.30
  41.5 28.3 %while.23 = (s32[]{:T(128)}, bf16[128,768]{1,0:T(8,128)(2,1)S(1)}, f32[512,768]{1,0:T(8,128)S(1)}, f32[512]{0:T(512)S(1)}, s32[]{:T(128)}, /*index=5*/s32[4]{0:T...) while((s32[]{:T(128)}, bf16[128,768]{1,0:T(8,128)(2,1)S(1)}, ...), condition=%wide.region_7.8_spmd.clone.clone, body=%wide.region_4.7_spmd.clone.clone.sunk | while | flops 203260192 | bytes 6246334 | solution.py:87
  41.5 1.5 collective-permute-start
  43.1 0.6 dynamic_slice.49
  43.6 1.4 compare_select_fusion.4
  45.1 5.5 %collective-permute-done = bf16[128,768]{1,0:T(8,128)(2,1)S(1)} collective-permute-done((bf16[128,768]{1,0:T(8,128)(2,1)S(1)}, bf16[128,768]{1,0:T(8,128)(2,1)S(1)}, u32[]{:S(2)}, u32[]{:S(2)}) %collective-permute-start) | collective-permute-done | bytes 196640 | tf_op jit(solution)/shard_map/while/body/eval_jaxpr/ppermute | solution.py:12
  50.6 0.4 fusion.62
  51.1 0.6 convolution_add_fusion.2
  51.8 0.6 dynamic_slice.49
  52.4 1.4 compare_select_fusion.4
  53.8 6.1 %collective-permute-done = bf16[128,768]{1,0:T(8,128)(2,1)S(1)} collective-permute-done((bf16[128,768]{1,0:T(8,128)(2,1)S(1)}, bf16[128,768]{1,0:T(8,128)(2,1)S(1)}, u32[]{:S(2)}, u32[]{:S(2)}) %collective-permute-start) | collective-permute-done | bytes 196640 | tf_op jit(solution)/shard_map/while/body/eval_jaxpr/ppermute | solution.py:12
  60.5 0.6 convolution_add_fusion.2
  61.2 0.6 dynamic_slice.49
  61.8 1.4 compare_select_fusion.4
  63.2 5.4 %collective-permute-done = bf16[128,768]{1,0:T(8,128)(2,1)S(1)} collective-permute-done((bf16[128,768]{1,0:T(8,128)(2,1)S(1)}, bf16[128,768]{1,0:T(8,128)(2,1)S(1)}, u32[]{:S(2)}, u32[]{:S(2)}) %collective-permute-start) | collective-permute-done | bytes 196640 | tf_op jit(solution)/shard_map/while/body/eval_jaxpr/ppermute | solution.py:12
  69.2 0.6 convolution_add_fusion.2
  69.8 1.1 fusion.21
  71.1 20.9 %reduce-scatter.5.cloned.1.call-done = bf16[128,768]{1,0:T(8,128)(2,1)} async-done(((bf16[512,768]{1,0:T(8,128)(2,1)}), bf16[128,768]{1,0:T(8,128)(2,1)}) %reduce-scatter.5.cloned.1.call-update) | async-done | bytes 196624 | tf_op jit(solution)/shard_map/reduce_scatter | solution.py:90
  92.0 7.5 %all_gather.7 = bf16[256,768]{1,0:T(8,128)(2,1)S(1)} all-gather(bf16[128,768]{1,0:T(8,128)(2,1)} %reduce-scatter.5.cloned.1.call-done), channel_id=1, replica_groups=mesh['groups'=2,'loop'=4,'enc'=2,'rep'=2] {'enc'}, dimensions={0}, use_global_device_ids=true | all-gather | bytes 589824 | tf_op jit(solution)/shard_map/all_gather | solution.py:93
  99.5 1.4 convolution_bitcast_fusion
  100.9 1.1 convolution_convert_fusion
  102.0 58.8 %all-reduce.2.cloned.1.call-done = f32[384,768]{0,1:T(8,128)} async-done(((f32[384,768]{0,1:T(8,128)}), f32[384,768]{0,1:T(8,128)}) %all-reduce.2.cloned.1.call-update) | async-done | bytes 1179664 | tf_op jit(solution)/shard_map/psum | solution.py:103
  160.8 2.7 %copy.9 = f32[384,768]{1,0:T(8,128)} copy(f32[384,768]{0,1:T(8,128)} %all-reduce.2.cloned.1.call-done) | data formatting | bytes 2359296
  (29 shorter events, 2.4 us)
Async XLA Ops:
  7.2 1.1 copy-start
  7.2 3.3 %copy-start.2 = (s32[4]{0:T(128)S(1)}, s32[4]{0:T(128)}, u32[]{:S(2)}) copy-start(s32[4]{0:T(128)} %param.9) | copy-start | bytes 52
  7.2 23.8 %reduce-scatter.3.cloned.1.call-start = ((), (), s32[]{:S(2)}) async-start(), calls=%async_computation.2 | async-start | bytes 1179648 | tf_op jit(solution)/shard_map/reduce_scatter | solution.py:30
  10.4 81.6 %reduce-scatter.5.cloned.1.call-start = ((), (), s32[]{:S(2)}) async-start(), calls=%async_computation.3 | async-start | bytes 983040 | tf_op jit(solution)/shard_map/reduce_scatter | solution.py:90
  41.5 9.0 %collective-permute-start = (bf16[128,768]{1,0:T(8,128)(2,1)S(1)}, bf16[128,768]{1,0:T(8,128)(2,1)S(1)}, u32[]{:S(2)}, u32[]{:S(2)}) collective-permute-start(bf16[128,768]{1,0:T(8,128)(2,1)S(1)} %get-tuple-element.558), channel_id=1, source_target_pairs={{0,4},{4,8},{8,12},{12,0},{1,5},{5,9},{9,13},{13,1},{2,6},{6,10},{... | collective-permute-start | bytes 589832 | tf_op jit(solution)/shard_map/while/body/eval_jaxpr/ppermute | solution.py:12
  51.7 8.2 %collective-permute-start = (bf16[128,768]{1,0:T(8,128)(2,1)S(1)}, bf16[128,768]{1,0:T(8,128)(2,1)S(1)}, u32[]{:S(2)}, u32[]{:S(2)}) collective-permute-start(bf16[128,768]{1,0:T(8,128)(2,1)S(1)} %get-tuple-element.558), channel_id=1, source_target_pairs={{0,4},{4,8},{8,12},{12,0},{1,5},{5,9},{9,13},{13,1},{2,6},{6,10},{... | collective-permute-start | bytes 589832 | tf_op jit(solution)/shard_map/while/body/eval_jaxpr/ppermute | solution.py:12
  61.1 7.5 %collective-permute-start = (bf16[128,768]{1,0:T(8,128)(2,1)S(1)}, bf16[128,768]{1,0:T(8,128)(2,1)S(1)}, u32[]{:S(2)}, u32[]{:S(2)}) collective-permute-start(bf16[128,768]{1,0:T(8,128)(2,1)S(1)} %get-tuple-element.558), channel_id=1, source_target_pairs={{0,4},{4,8},{8,12},{12,0},{1,5},{5,9},{9,13},{13,1},{2,6},{6,10},{... | collective-permute-start | bytes 589832 | tf_op jit(solution)/shard_map/while/body/eval_jaxpr/ppermute | solution.py:12
  69.8 29.7 %copy-start.1 = (bf16[256,384]{1,0:T(8,128)(2,1)S(1)}, bf16[256,384]{1,0:T(8,128)(2,1)}, u32[]{:S(2)}) copy-start(bf16[256,384]{1,0:T(8,128)(2,1)} %param.6) | copy-start | bytes 589828
  71.0 89.8 %all-reduce.2.cloned.1.call-start = ((), (), s32[]{:S(2)}) async-start(), calls=%async_computation.4 | async-start | bytes 2359296 | tf_op jit(solution)/shard_map/psum | solution.py:103
Sparse Core Ops, SparseCore 0:
  10.8 20.1 reduce-scatter.2
  71.1 20.8 reduce-scatter.4
  101.1 59.6 all-reduce.1
where the time goes:
time: 170 us
  waiting for transfers between devices  114 us (67%)
  blocking collectives  15.7 us (9%)
  between operations  13.8 us (8%)
  other arithmetic  9.37 us (6%)
  matrix products  8.66 us (5%)
  local copies, waits for them, and re-layouts  6.9 us (4%)
  starting transfers between devices  1.78 us (1%)
    psum x1, waiting for transfers between devices, body(): head_grad = lax.psum(head_part, ('loop', 'rep'))  58.8 us
    reduce_scatter x1, waiting for transfers between devices, body(): lax.psum_scatter(grad_block.astype(jnp.bfloat16), ('enc', 'rep'), scatter...  20.9 us
    ppermute x3, waiting for transfers between devices, passed_along(): return lax.ppermute(value, axis, pairs)  17 us
    reduce_scatter x1, waiting for transfers between devices, body(): lax.psum_scatter(jnp.dot(rows, head_weight, preferred_element_type=jnp.fl...  16.8 us
    all_gather x1, blocking collectives, body(): block_feats = lax.all_gather(own_feats, ('enc', 'rep'), axis=0, tiled=True)  8.2 us
    all_gather x1, blocking collectives, body(): piece = lax.all_gather(own_grad, 'enc', axis=0, tiled=True)  7.51 us
    select_n x4, other arithmetic, tile(): piece_coef = jnp.where(piece_offsets < anchor_count, piece_coef, 0.0)  5.68 us
    unnamed x7, local copies, waits for them, and re-layouts  3.67 us
  transfers between devices with their start and end apart: 6, of which 6 were waited for; matrix products, arithmetic and copies ran while one was open for 6% of the time, Pallas kernels for 0%

commit v1 on v0

--- a/solution.py
+++ b/solution.py
@@ -4,6 +4,19 @@
 from jax.sharding import PartitionSpec as P
 
 EPSILON = 1e-06
+
+
+def ring_gather(x, axis, dim):
+    ways = lax.axis_size(axis)
+    up = [(d, (d + 1) % ways) for d in range(ways)]
+    down = [(d, (d - 1) % ways) for d in range(ways)]
+    earlier, later = ([x], [x])
+    for _ in range(ways // 2):
+        earlier.append(lax.ppermute(earlier[-1], axis, up))
+    for _ in range((ways - 1) // 2):
+        later.append(lax.ppermute(later[-1], axis, down))
+    line = jnp.concatenate([*earlier[::-1], *later[1:]], axis=dim)
+    return jnp.roll(line, (lax.axis_index(axis) - ways // 2) * x.shape[dim], axis=dim)
 
 
 def passed_along(value, axis, steps):
@@ -33,7 +46,7 @@
         scatter_dimension=0,
         tiled=True,
     ).astype(jnp.bfloat16)
-    block_feats = lax.all_gather(own_feats, ("enc", "rep"), axis=0, tiled=True)
+    block_feats = ring_gather(own_feats, ("enc", "rep"), 0)
     block_norms = jnp.sum(jnp.square(block_feats.astype(jnp.float32)), axis=1)
     offsets = (
         jnp.arange(rep_size, dtype=jnp.int32)[None, :, None] * share_rows

time: 170 us -> 176 us (1.035)
  waiting for transfers between devices: 114 us -> 125 us
  blocking collectives: 15.7 us -> 7.53 us
  starting transfers between devices: 1.78 us -> 3.57 us
    all_gather x1 -> x0, blocking collectives: 8.2 us -> none  [body(): block_feats = lax.all_gather(own_feats, ('enc', 'rep'), axis=0, tiled=True)]
    ppermute x0 -> x3, waiting for transfers between devices: none -> 8.13 us  [the longest x2 6.27 us: ring_gather(): earlier.append(lax.ppermute(earlier[-1], axis, up))]
    reduce_scatter x1, waiting for transfers between devices: 16.8 us -> 19.2 us  [body(): lax.psum_scatter(jnp.dot(rows, head_weight, preferred_element_type=jnp.fl...]
    ppermute x0 -> x3, starting transfers between devices: none -> 1.8 us  [the longest x1 1.74 us: ring_gather(): later.append(lax.ppermute(later[-1], axis, down))]
    unnamed x7 -> x14, local copies, waits for them, and re-layouts: 3.67 us -> 3.77 us
  transfers between devices with their start and end apart: 6 -> 9, of which waited for: 6 -> 9; matrix products, arithmetic and copies ran while one was open for 6% -> 6% of each run, Pallas kernels for 0% -> 0%
where the time goes in v1:
time: 176 us; the launch traced here: 175 us
  waiting for transfers between devices  125 us (71%)
  between operations  13.9 us (8%)
  other arithmetic  9.38 us (5%)
  matrix products  8.66 us (5%)
  blocking collectives  7.53 us (4%)
  local copies, waits for them, and re-layouts  7.19 us (4%)
  starting transfers between devices  3.57 us (2%)
    psum x1, waiting for transfers between devices, body(): head_grad = lax.psum(head_part, ('loop', 'rep'))  58.7 us
    reduce_scatter x1, waiting for transfers between devices, body(): lax.psum_scatter(grad_block.astype(jnp.bfloat16), ('enc', 'rep'), scatter...  21.7 us
    reduce_scatter x1, waiting for transfers between devices, body(): lax.psum_scatter(jnp.dot(rows, head_weight, preferred_element_type=jnp.fl...  19.2 us
    ppermute x3, waiting for transfers between devices, passed_along(): return lax.ppermute(value, axis, pairs)  17.3 us
    all_gather x1, blocking collectives, body(): piece = lax.all_gather(own_grad, 'enc', axis=0, tiled=True)  7.53 us
    ppermute x2, waiting for transfers between devices, ring_gather(): earlier.append(lax.ppermute(earlier[-1], axis, up))  6.27 us
    select_n x4, other arithmetic, tile(): piece_coef = jnp.where(piece_offsets < anchor_count, piece_coef, 0.0)  5.74 us
    unnamed x14, local copies, waits for them, and re-layouts  3.77 us
  transfers between devices with their start and end apart: 9, of which 9 were waited for; matrix products, arithmetic and copies ran while one was open for 6% of the time, Pallas kernels for 0%

profile of v1, /device:TPU:0, one launch (start us, length us, event | category | flops | bytes accessed | tf_op | source)
XLA Modules:
  0.0 175.4 jit_solution(8248045239394809225)
XLA Ops:
  7.2 1.0 copy-done
  8.2 2.2 %fusion.40 = f32[256,768]{1,0:T(8,128)} fusion(bf16[256,384]{1,0:T(8,128)(2,1)} %param.6, bf16[384,768]{1,0:T(8,128)(2,1)S(1)} %copy-done), kind=kOutput, calls=%fused_computation.65 | convolution fusion | flops 150994944 | bytes 1572864 | tf_op jit(solution)/shard_map/dot_general | solution.py:44
  10.5 0.6 dynamic_slice.41
  11.1 0.8 dynamic_slice.43
  11.9 19.2 %reduce-scatter.3.cloned.1.call-done = f32[128,768]{1,0:T(8,128)} async-done(((f32[256,768]{1,0:T(8,128)}), f32[128,768]{1,0:T(8,128)}) %reduce-scatter.3.cloned.1.call-update) | async-done | bytes 393232 | tf_op jit(solution)/shard_map/reduce_scatter | solution.py:43
  31.0 1.1 multiply_reduce_fusion.1
  32.3 5.0 %collective-permute-done.1 = bf16[128,768]{1,0:T(8,128)(2,1)S(1)} collective-permute-done((bf16[128,768]{1,0:T(8,128)(2,1)S(1)}, bf16[128,768]{1,0:T(8,128)(2,1)S(1)}, u32[]{:S(2)}, u32[]{:S(2)}) %collective-permute-start.1) | collective-permute-done | bytes 196640 | tf_op jit(solution)/shard_map/ppermute | solution.py:15
  37.3 0.7 compare_select_fusion.1
  38.0 1.4 compare_select_fusion.2
  39.4 1.7 collective-permute-start.3
  41.1 1.3 collective-permute-done.2
  42.4 1.9 %collective-permute-done.3 = bf16[128,768]{1,0:T(8,128)(2,1)S(1)} collective-permute-done((bf16[128,768]{1,0:T(8,128)(2,1)S(1)}, bf16[128,768]{1,0:T(8,128)(2,1)S(1)}, u32[]{:S(2)}, u32[]{:S(2)}) %collective-permute-start.3) | collective-permute-done | bytes 196640 | tf_op jit(solution)/shard_map/ppermute | solution.py:17
  45.6 29.0 %while.23 = (s32[]{:T(128)}, bf16[128,768]{1,0:T(8,128)(2,1)S(1)}, f32[512,768]{1,0:T(8,128)S(1)}, f32[512]{0:T(512)S(1)}, s32[]{:T(128)}, /*index=5*/s32[4]{0:T...) while((s32[]{:T(128)}, bf16[128,768]{1,0:T(8,128)(2,1)S(1)}, ...), condition=%wide.region_7.8_spmd.clone.clone, body=%wide.region_4.7_spmd.clone.clone.sunk | while | flops 203260192 | bytes 6246334 | solution.py:100
  45.6 1.5 collective-permute-start
  47.1 0.7 dynamic_slice.56
  47.8 1.5 compare_select_fusion.4
  49.3 5.6 %collective-permute-done = bf16[128,768]{1,0:T(8,128)(2,1)S(1)} collective-permute-done((bf16[128,768]{1,0:T(8,128)(2,1)S(1)}, bf16[128,768]{1,0:T(8,128)(2,1)S(1)}, u32[]{:S(2)}, u32[]{:S(2)}) %collective-permute-start) | collective-permute-done | bytes 196640 | tf_op jit(solution)/shard_map/while/body/eval_jaxpr/ppermute | solution.py:25
  56.2 0.7 dynamic_slice.56
  56.8 1.5 compare_select_fusion.4
  58.3 6.3 %collective-permute-done = bf16[128,768]{1,0:T(8,128)(2,1)S(1)} collective-permute-done((bf16[128,768]{1,0:T(8,128)(2,1)S(1)}, bf16[128,768]{1,0:T(8,128)(2,1)S(1)}, u32[]{:S(2)}, u32[]{:S(2)}) %collective-permute-start) | collective-permute-done | bytes 196640 | tf_op jit(solution)/shard_map/while/body/eval_jaxpr/ppermute | solution.py:25
  65.2 0.6 convolution_add_fusion.2
  65.9 0.7 dynamic_slice.56
  66.5 1.5 compare_select_fusion.4
  68.0 5.4 %collective-permute-done = bf16[128,768]{1,0:T(8,128)(2,1)S(1)} collective-permute-done((bf16[128,768]{1,0:T(8,128)(2,1)S(1)}, bf16[128,768]{1,0:T(8,128)(2,1)S(1)}, u32[]{:S(2)}, u32[]{:S(2)}) %collective-permute-start) | collective-permute-done | bytes 196640 | tf_op jit(solution)/shard_map/while/body/eval_jaxpr/ppermute | solution.py:25
  74.0 0.6 convolution_add_fusion.2
  74.6 1.1 fusion.21
  75.8 21.7 %reduce-scatter.5.cloned.1.call-done = bf16[128,768]{1,0:T(8,128)(2,1)} async-done(((bf16[512,768]{1,0:T(8,128)(2,1)}), bf16[128,768]{1,0:T(8,128)(2,1)}) %reduce-scatter.5.cloned.1.call-update) | async-done | bytes 196624 | tf_op jit(solution)/shard_map/reduce_scatter | solution.py:103
  97.5 7.5 %all_gather.3 = bf16[256,768]{1,0:T(8,128)(2,1)S(1)} all-gather(bf16[128,768]{1,0:T(8,128)(2,1)} %reduce-scatter.5.cloned.1.call-done), channel_id=1, replica_groups=mesh['groups'=2,'loop'=4,'enc'=2,'rep'=2] {'enc'}, dimensions={0}, use_global_device_ids=true | all-gather | bytes 589824 | tf_op jit(solution)/shard_map/all_gather | solution.py:106
  105.1 1.4 convolution_bitcast_fusion
  106.5 1.1 convolution_convert_fusion
  107.6 58.7 %all-reduce.2.cloned.1.call-done = f32[384,768]{0,1:T(8,128)} async-done(((f32[384,768]{0,1:T(8,128)}), f32[384,768]{0,1:T(8,128)}) %all-reduce.2.cloned.1.call-update) | async-done | bytes 1179664 | tf_op jit(solution)/shard_map/psum | solution.py:116
  166.2 2.7 %copy.9 = f32[384,768]{1,0:T(8,128)} copy(f32[384,768]{0,1:T(8,128)} %all-reduce.2.cloned.1.call-done) | data formatting | bytes 2359296
  (42 shorter events, 4.1 us)
Async XLA Ops:
  7.2 1.1 copy-start
  7.2 3.3 %copy-start.2 = (s32[4]{0:T(128)S(1)}, s32[4]{0:T(128)}, u32[]{:S(2)}) copy-start(s32[4]{0:T(128)} %param.9) | copy-start | bytes 52
  7.2 23.8 %reduce-scatter.3.cloned.1.call-start = ((), (), s32[]{:S(2)}) async-start(), calls=%async_computation.2 | async-start | bytes 1179648 | tf_op jit(solution)/shard_map/reduce_scatter | solution.py:43
  10.4 87.1 %reduce-scatter.5.cloned.1.call-start = ((), (), s32[]{:S(2)}) async-start(), calls=%async_computation.3 | async-start | bytes 983040 | tf_op jit(solution)/shard_map/reduce_scatter | solution.py:103
  32.1 5.1 %collective-permute-start.1 = (bf16[128,768]{1,0:T(8,128)(2,1)S(1)}, bf16[128,768]{1,0:T(8,128)(2,1)S(1)}, u32[]{:S(2)}, u32[]{:S(2)}) collective-permute-start(bf16[128,768]{1,0:T(8,128)(2,1)S(1)} %get-tuple-element.543), channel_id=1, source_target_pairs={{0,1},{1,2},{2,3},{3,0},{4,5},{5,6},{6,7},{7,4},{8,9},{9,10},{10,1... | collective-permute-start | bytes 589832 | tf_op jit(solution)/shard_map/ppermute | solution.py:15
  37.3 5.1 %collective-permute-start.2 = (bf16[128,768]{1,0:T(8,128)(2,1)S(1)}, bf16[128,768]{1,0:T(8,128)(2,1)S(1)}, u32[]{:S(2)}, u32[]{:S(2)}) collective-permute-start(bf16[128,768]{1,0:T(8,128)(2,1)S(1)} %collective-permute-done.1), channel_id=1, source_target_pairs={{0,1},{1,2},{2,3},{3,0},{4,5},{5,6},{6,7},{7,4},{8,9},{9,10},{10,1... | collective-permute-start | bytes 589832 | tf_op jit(solution)/shard_map/ppermute | solution.py:15
  39.4 4.9 %collective-permute-start.3 = (bf16[128,768]{1,0:T(8,128)(2,1)S(1)}, bf16[128,768]{1,0:T(8,128)(2,1)S(1)}, u32[]{:S(2)}, u32[]{:S(2)}) collective-permute-start(bf16[128,768]{1,0:T(8,128)(2,1)S(1)} %get-tuple-element.543), channel_id=1, source_target_pairs={{0,3},{1,0},{2,1},{3,2},{4,7},{5,4},{6,5},{7,6},{8,11},{9,8},{10,9... | collective-permute-start | bytes 589832 | tf_op jit(solution)/shard_map/ppermute | solution.py:17
  45.6 9.3 %collective-permute-start = (bf16[128,768]{1,0:T(8,128)(2,1)S(1)}, bf16[128,768]{1,0:T(8,128)(2,1)S(1)}, u32[]{:S(2)}, u32[]{:S(2)}) collective-permute-start(bf16[128,768]{1,0:T(8,128)(2,1)S(1)} %get-tuple-element.560), channel_id=1, source_target_pairs={{0,4},{4,8},{8,12},{12,0},{1,5},{5,9},{9,13},{13,1},{2,6},{6,10},{... | collective-permute-start | bytes 589832 | tf_op jit(solution)/shard_map/while/body/eval_jaxpr/ppermute | solution.py:25
  56.1 8.5 %collective-permute-start = (bf16[128,768]{1,0:T(8,128)(2,1)S(1)}, bf16[128,768]{1,0:T(8,128)(2,1)S(1)}, u32[]{:S(2)}, u32[]{:S(2)}) collective-permute-start(bf16[128,768]{1,0:T(8,128)(2,1)S(1)} %get-tuple-element.560), channel_id=1, source_target_pairs={{0,4},{4,8},{8,12},{12,0},{1,5},{5,9},{9,13},{13,1},{2,6},{6,10},{... | collective-permute-start | bytes 589832 | tf_op jit(solution)/shard_map/while/body/eval_jaxpr/ppermute | solution.py:25
  65.8 7.6 %collective-permute-start = (bf16[128,768]{1,0:T(8,128)(2,1)S(1)}, bf16[128,768]{1,0:T(8,128)(2,1)S(1)}, u32[]{:S(2)}, u32[]{:S(2)}) collective-permute-start(bf16[128,768]{1,0:T(8,128)(2,1)S(1)} %get-tuple-element.560), channel_id=1, source_target_pairs={{0,4},{4,8},{8,12},{12,0},{1,5},{5,9},{9,13},{13,1},{2,6},{6,10},{... | collective-permute-start | bytes 589832 | tf_op jit(solution)/shard_map/while/body/eval_jaxpr/ppermute | solution.py:25
  74.6 30.5 %copy-start.1 = (bf16[256,384]{1,0:T(8,128)(2,1)S(1)}, bf16[256,384]{1,0:T(8,128)(2,1)}, u32[]{:S(2)}) copy-start(bf16[256,384]{1,0:T(8,128)(2,1)} %param.6) | copy-start | bytes 589828
  75.8 90.5 %all-reduce.2.cloned.1.call-start = ((), (), s32[]{:S(2)}) async-start(), calls=%async_computation.4 | async-start | bytes 2359296 | tf_op jit(solution)/shard_map/psum | solution.py:116
Sparse Core Ops, SparseCore 0:
  10.8 20.1 reduce-scatter.2
  75.9 21.6 reduce-scatter.4
  106.6 59.5 all-reduce.1
